TPU v7x, 32 devices: a whole 2x2x4 slice. The times are simulated.
32 devices in a mesh: ctx: 8 (over y, x, core), chan: 4 (over z).
Axes of the slice: x: 2, y: 2, z: 4, core: 2. Of those that a mesh axis runs over, the one named last changes fastest.
Arguments:
- stream: bfloat16 [1024, 8192], P('ctx', 'chan'), may hold values from -64 to 64, as said below
- seg_ids: int32 [1024], P('ctx'), may hold values from 0 to 7, never falling along the last dimension, each value on 1 to 256 neighbouring positions
- mr_gain: float32 [8192], P('chan'), may hold values from 0.1 to 1.9
- mr_filter: bfloat16 [8192, 128], P('chan'), may hold values from -0.5 to 0.5
- li_gain: float32 [8192], P('chan'), may hold values from 0.1 to 1.9
- decay_rates: float32 [8192, 16], P('chan'), may hold values from 0 to 1, as said below
- residues: float32 [8192, 16], P('chan'), may hold values from -1.5 to 1.5
Outputs:
- result: bfloat16 [1024, 8192], P('ctx', 'chan')
Inputs may be any that keep to these rules, and one draw needn't show every extreme that they name: `seg_ids`: document numbers never fall along the context; each document holds at most 256 positions, and one holds exactly that many. `stream`: activations. `decay_rates`: positive rates.
All inputs are finite; a program needn't handle non-finite values.
Results may differ from a plain program's by a relative error of at most 0.0064.
Values may be sent and summed in bfloat16 or wider, within the bound.
A program may use at most 128 MiB of HBM per device.

v0:
```python
from functools import partial

import jax
import jax.numpy as jnp
from jax import lax
from jax.sharding import PartitionSpec as P

EPSILON = 1e-06
HIGHEST = lax.Precision.HIGHEST


def from_behind(block, axis, distance):
    devices = range(lax.axis_size(axis))
    route = [(i - distance, i) for i in devices if i - distance in devices]
    return lax.ppermute(block, axis, route)


def entering(array, axis, combine, identity):
    devices, place = (lax.axis_size(axis), lax.axis_index(axis))
    everything = jax.tree.map(lambda part: lax.all_gather(part, axis), array)
    start = jax.tree.map(
        lambda part, zero: jnp.broadcast_to(jnp.asarray(zero, part.dtype), part.shape),
        array,
        identity,
    )

    def hop(k, before):
        reached = k < place
        new = combine(before, jax.tree.map(lambda part: part[k], everything))
        return jax.tree.map(lambda a, b: jnp.where(reached, a, b), new, before)

    return lax.fori_loop(0, devices, hop, start)


def depthwise(widened, filter_taps):
    rim_rows = filter_taps.shape[1] - 1
    count = widened.shape[0] - rim_rows
    taps_float = filter_taps.astype(jnp.float32)
    total = jnp.zeros((count, filter_taps.shape[0]), jnp.float32)
    for lag in range(rim_rows + 1):
        rows = widened[rim_rows - lag : rim_rows - lag + count].astype(jnp.float32)
        total = total + rows * taps_float[:, lag]
    return total


def local_pass(group_items, seg_ids, block_size, need_end):
    inputs, rate_group, coef_group = group_items
    offsets = jnp.arange(block_size)
    offset_float = offsets.astype(jnp.float32)
    lag_matrix = offsets[:, None] - offsets[None, :]
    causal = lag_matrix >= 0
    lag_float = jnp.where(causal, lag_matrix, 0).astype(jnp.float32)
    toeplitz = jnp.zeros((rate_group.shape[0], block_size, block_size), jnp.float32)
    for mode in range(rate_group.shape[1]):
        toeplitz = toeplitz + coef_group[:, mode, None, None] * jnp.exp(
            -rate_group[:, mode, None, None] * lag_float[None]
        )
    tail_terms = jnp.exp(-rate_group[:, :, None] * (block_size - 1.0 - offset_float))
    same_doc = (seg_ids[:, None] == seg_ids[None, :]) & causal
    masked_kernel = jnp.where(same_doc[None], toeplitz, 0.0)
    outcome = jnp.einsum("gts,sg->tg", masked_kernel, inputs, precision=HIGHEST)
    pieces = [outcome]
    ending = seg_ids == seg_ids[block_size - 1]
    fresh = jnp.einsum(
        "gms,sg->gm", tail_terms, jnp.where(ending[:, None], inputs, 0.0), precision=HIGHEST
    )
    return (jnp.concatenate(pieces, axis=0), fresh)


def correction(group_items, alive):
    state_in, rate_group, coef_group = group_items
    length = alive.shape[0]
    position_float = jnp.arange(length).astype(jnp.float32)
    lead_terms = coef_group[:, :, None] * jnp.exp(-rate_group[:, :, None] * (position_float + 1.0))
    carry_terms = jnp.einsum("gmt,gm->tg", lead_terms, state_in, precision=HIGHEST)
    return jnp.where(alive[:, None], carry_terms, 0.0)


def combine_states(earlier, later):
    return (earlier[0] * later[0], later[0] * earlier[1] + later[1])


def per_device(stream, seg_ids, mr_gain, mr_filter, li_gain, decay_rates, residues):
    length, channels = stream.shape
    full_width = channels * lax.axis_size("chan")
    rim_rows = mr_filter.shape[1] - 1
    xfloat = stream.astype(jnp.float32)
    squares = jnp.sum(xfloat * xfloat, axis=1)
    last_id = seg_ids[length - 1 :]
    sum_total = lax.psum(squares, "chan")
    inverse = lax.rsqrt(sum_total / full_width + EPSILON)
    normed = (xfloat * inverse[:, None] * mr_gain).astype(jnp.bfloat16)
    earlier_rows, earlier_id = from_behind((normed[length - rim_rows :], last_id), "ctx", 1)
    widened = jnp.concatenate([earlier_rows, normed])
    mixed = depthwise(widened, mr_filter)
    first = (xfloat + normed.astype(jnp.float32) * mixed).astype(jnp.bfloat16)
    first_float = first.astype(jnp.float32)
    second_total = lax.psum(jnp.sum(first_float * first_float, axis=1), "chan")
    second = first_float * lax.rsqrt(second_total / full_width + EPSILON)[:, None] * li_gain
    coefs = residues * jnp.sqrt(-jnp.expm1(-2.0 * decay_rates))
    modes = decay_rates.shape[1]
    group_size = min(128, channels)
    group_count = channels // group_size
    block_size = min(128, length)
    grouped_inputs = second.reshape(length, group_count, group_size).transpose(1, 0, 2)
    grouped_rates = decay_rates.reshape(group_count, group_size, modes)
    grouped_coefs = coefs.reshape(group_count, group_size, modes)
    alive = seg_ids == earlier_id[0]
    through_all = seg_ids[length - 1] == earlier_id[0]
    shard_decay = jnp.where(through_all, jnp.exp(-decay_rates * length), 0.0)
    local_terms, end_groups = lax.map(
        partial(local_pass, seg_ids=seg_ids, block_size=block_size, need_end=True),
        (grouped_inputs, grouped_rates, grouped_coefs),
    )
    end_state = end_groups.reshape(channels, modes)
    prefix = entering(
        (shard_decay, end_state),
        "ctx",
        combine_states,
        (jnp.ones_like(shard_decay), jnp.zeros_like(end_state)),
    )
    state_in = prefix[1].reshape(group_count, group_size, modes)
    carry_terms = lax.map(
        partial(correction, alive=alive), (state_in, grouped_rates, grouped_coefs)
    )
    longconv = (local_terms + carry_terms).transpose(1, 0, 2).reshape(length, channels)
    return (first_float + second * longconv).astype(jnp.bfloat16)


def solution(mesh):
    placed = (
        P("ctx", "chan"),
        P("ctx"),
        P("chan"),
        P("chan", None),
        P("chan"),
        P("chan", None),
        P("chan", None),
    )
    return jax.shard_map(
        per_device, mesh=mesh, in_specs=placed, out_specs=P("ctx", "chan"), check_vma=False
    )
```

profile of v0, /device:TPU:4, one launch (start us, length us, event | category | flops | bytes accessed | tf_op | source)
XLA Modules:
  0.0 717.7 jit_solution(9648830753937740888)
XLA Ops:
  6.5 1.2 fusion.46
  7.8 12.0 %psum.14 = f32[128]{0:T(128)S(1)} all-reduce(f32[128]{0:T(128)S(1)} %fusion.46), channel_id=1, replica_groups=mesh['ctx'=8,'chan'=4] {'chan'}, use_global_device_ids=true, to_apply=%region_1.0 | all-reduce | flops 128 | bytes 1024 | tf_op jit(solution)/shard_map/psum | solution.py:90
  19.8 1.3 fusion.48
  21.2 1.9 collective-permute-start
  23.7 3.5 collective-permute-start.1
  27.3 10.9 %slice_reduce_fusion.127 = (f32[2048]{0:T(1024)}, f32[2048]{0:T(1024)}, f32[2048]{0:T(1024)}, f32[2048]{0:T(1024)}, f32[2048]{0:T(1024)}, /*index=5*/f32[2048]{0...) fusion(f32[2048,128]{1,0:T(8,128)S(1)} %convert_element_type.457), kind=kLoop, calls=%fused_computation.495 | loop fusion | bytes 311296 | tf_op jit(solution)/shard_map/slice | solution.py:42
  38.2 11.2 %slice_reduce_fusion.124 = (f32[2048]{0:T(1024)}, f32[2048]{0:T(1024)}, f32[2048]{0:T(1024)}, f32[2048]{0:T(1024)}, f32[2048]{0:T(1024)}, /*index=5*/f32[2048]{0...) fusion(f32[2048,128]{1,0:T(8,128)S(1)} %convert_element_type.457), kind=kLoop, calls=%fused_computation.492 | loop fusion | bytes 311296 | tf_op jit(solution)/shard_map/slice | solution.py:42
  49.4 11.7 %slice_reduce_fusion.123 = (f32[2048]{0:T(1024)}, f32[2048]{0:T(1024)}, f32[2048]{0:T(1024)}, f32[2048]{0:T(1024)}, f32[2048]{0:T(1024)}, /*index=5*/f32[2048]{0...) fusion(f32[2048,128]{1,0:T(8,128)S(1)} %convert_element_type.457), kind=kLoop, calls=%fused_computation.491 | loop fusion | bytes 311296 | tf_op jit(solution)/shard_map/slice | solution.py:42
  61.0 11.1 %slice_reduce_fusion.122 = (f32[2048]{0:T(1024)}, f32[2048]{0:T(1024)}, f32[2048]{0:T(1024)}, f32[2048]{0:T(1024)}, f32[2048]{0:T(1024)}, /*index=5*/f32[2048]{0...) fusion(f32[2048,128]{1,0:T(8,128)S(1)} %convert_element_type.457), kind=kLoop, calls=%fused_computation.490 | loop fusion | bytes 311296 | tf_op jit(solution)/shard_map/slice | solution.py:42
  72.2 11.3 %slice_reduce_fusion.121 = (f32[2048]{0:T(1024)}, f32[2048]{0:T(1024)}, f32[2048]{0:T(1024)}, f32[2048]{0:T(1024)}, f32[2048]{0:T(1024)}, /*index=5*/f32[2048]{0...) fusion(f32[2048,128]{1,0:T(8,128)S(1)} %convert_element_type.457), kind=kLoop, calls=%fused_computation.489 | loop fusion | bytes 311296 | tf_op jit(solution)/shard_map/slice | solution.py:42
  83.5 11.3 %slice_reduce_fusion.120 = (f32[2048]{0:T(1024)}, f32[2048]{0:T(1024)}, f32[2048]{0:T(1024)}, f32[2048]{0:T(1024)}, f32[2048]{0:T(1024)}, /*index=5*/f32[2048]{0...) fusion(f32[2048,128]{1,0:T(8,128)S(1)} %convert_element_type.457), kind=kLoop, calls=%fused_computation.488 | loop fusion | bytes 311296 | tf_op jit(solution)/shard_map/slice | solution.py:42
  94.8 8.2 %slice_reduce_fusion.119 = (f32[2048]{0:T(1024)}, f32[2048]{0:T(1024)}, f32[2048]{0:T(1024)}, f32[2048]{0:T(1024)}, f32[2048]{0:T(1024)}, /*index=5*/f32[2048]{0...) fusion(f32[2048,128]{1,0:T(8,128)S(1)} %convert_element_type.457), kind=kLoop, calls=%fused_computation.487 | loop fusion | bytes 229376 | tf_op jit(solution)/shard_map/slice | solution.py:42
  105.2 1.4 fusion.175
  106.6 1.2 fusion.166
  107.8 1.3 fusion.157
  109.1 2.5 fusion.148
  111.6 2.6 fusion.139
  114.2 2.5 fusion.130
  116.8 2.5 fusion.121
  119.2 2.5 fusion.112
  121.8 2.4 fusion.103
  124.1 2.5 fusion.94
  126.6 2.5 fusion.85
  129.1 2.5 fusion.76
  131.5 2.5 fusion.67
  134.0 2.4 fusion.58
  137.6 39.2 %fusion.50 = (f32[128]{0:T(128)S(1)}, bf16[128,2048]{1,0:T(8,128)(2,1)S(1)}) fusion(f32[2048]{0:T(1024)S(1)} %copy-done.7, bf16[128,2048]{1,0:T(8,128)(2,1)S(1)} %get-tuple-element.560, f32[2048]{0:T(1024)S(1)} %copy-done.8, bf16[128,2048]{1,0:T(8,128)(2,1)S(1)} %get-tuple-element.561, f32[2048]{0:T(1024)S(1)} %copy-done.9, ...), kind=kLoop, calls=%fused_computation.362 | loop fusion | flops 101187456 | bytes 70238720 | tf_op jit(solution)/shard_map/reduce_sum | solution.py:98
  176.8 8.5 %psum.15 = f32[128]{0:T(128)S(1)} all-reduce(f32[128]{0:T(128)S(1)} %get-tuple-element.399), channel_id=1, replica_groups=mesh['ctx'=8,'chan'=4] {'chan'}, use_global_device_ids=true, to_apply=%region_3.0 | all-reduce | flops 128 | bytes 1024 | tf_op jit(solution)/shard_map/psum | solution.py:98
  185.7 467.0 %while.36 = (s32[]{:T(128)}, f32[16,128,128]{2,1,0:T(8,128)S(1)}, f32[16,128,16]{1,0,2:T(8,128)S(1)}, f32[16,128,128]{2,1,0:T(8,128)S(1)}, s32[128]{0:T(128)S(1)...) while((s32[]{:T(128)}, f32[16,128,128]{2,1,0:T(8,128)S(1)}, ...), condition=%wide.region_5.6_spmd, body=%wide.region_4.5_spmd.sunk | while | flops 105777536 | bytes 1304969 | solution.py:111
  186.0 26.5 %multiply_reduce_fusion.6 = f32[128,128]{1,0:T(8,128)S(1)} fusion(f32[128,128]{1,0:T(8,128)S(1)} %copy.91, f32[128]{0:T(128)S(1)} %get-tuple-element.701, f32[128]{0:T(128)S(1)} %get-tuple-element.702, f32[128]{0:T(128)S(1)} %get-tuple-element.703, f32[128]{0:T(128)S(1)} %get-tuple-element.704, f32[128]{0:T(128)S(1)} %get-tuple-element.705, ...), kind=kLoop, calls=%fused_computation.5.clone.1 | loop fusion | flops 104841216 | bytes 229376 | tf_op jit(solution)/shard_map/while
  215.2 26.5 %multiply_reduce_fusion.6 = f32[128,128]{1,0:T(8,128)S(1)} fusion(f32[128,128]{1,0:T(8,128)S(1)} %copy.91, f32[128]{0:T(128)S(1)} %get-tuple-element.701, f32[128]{0:T(128)S(1)} %get-tuple-element.702, f32[128]{0:T(128)S(1)} %get-tuple-element.703, f32[128]{0:T(128)S(1)} %get-tuple-element.704, f32[128]{0:T(128)S(1)} %get-tuple-element.705, ...), kind=kLoop, calls=%fused_computation.5.clone.1 | loop fusion | flops 104841216 | bytes 229376 | tf_op jit(solution)/shard_map/while
  244.4 26.5 %multiply_reduce_fusion.6 = f32[128,128]{1,0:T(8,128)S(1)} fusion(f32[128,128]{1,0:T(8,128)S(1)} %copy.91, f32[128]{0:T(128)S(1)} %get-tuple-element.701, f32[128]{0:T(128)S(1)} %get-tuple-element.702, f32[128]{0:T(128)S(1)} %get-tuple-element.703, f32[128]{0:T(128)S(1)} %get-tuple-element.704, f32[128]{0:T(128)S(1)} %get-tuple-element.705, ...), kind=kLoop, calls=%fused_computation.5.clone.1 | loop fusion | flops 104841216 | bytes 229376 | tf_op jit(solution)/shard_map/while
  273.5 26.5 %multiply_reduce_fusion.6 = f32[128,128]{1,0:T(8,128)S(1)} fusion(f32[128,128]{1,0:T(8,128)S(1)} %copy.91, f32[128]{0:T(128)S(1)} %get-tuple-element.701, f32[128]{0:T(128)S(1)} %get-tuple-element.702, f32[128]{0:T(128)S(1)} %get-tuple-element.703, f32[128]{0:T(128)S(1)} %get-tuple-element.704, f32[128]{0:T(128)S(1)} %get-tuple-element.705, ...), kind=kLoop, calls=%fused_computation.5.clone.1 | loop fusion | flops 104841216 | bytes 229376 | tf_op jit(solution)/shard_map/while
  302.7 26.5 %multiply_reduce_fusion.6 = f32[128,128]{1,0:T(8,128)S(1)} fusion(f32[128,128]{1,0:T(8,128)S(1)} %copy.91, f32[128]{0:T(128)S(1)} %get-tuple-element.701, f32[128]{0:T(128)S(1)} %get-tuple-element.702, f32[128]{0:T(128)S(1)} %get-tuple-element.703, f32[128]{0:T(128)S(1)} %get-tuple-element.704, f32[128]{0:T(128)S(1)} %get-tuple-element.705, ...), kind=kLoop, calls=%fused_computation.5.clone.1 | loop fusion | flops 104841216 | bytes 229376 | tf_op jit(solution)/shard_map/while
  331.9 26.5 %multiply_reduce_fusion.6 = f32[128,128]{1,0:T(8,128)S(1)} fusion(f32[128,128]{1,0:T(8,128)S(1)} %copy.91, f32[128]{0:T(128)S(1)} %get-tuple-element.701, f32[128]{0:T(128)S(1)} %get-tuple-element.702, f32[128]{0:T(128)S(1)} %get-tuple-element.703, f32[128]{0:T(128)S(1)} %get-tuple-element.704, f32[128]{0:T(128)S(1)} %get-tuple-element.705, ...), kind=kLoop, calls=%fused_computation.5.clone.1 | loop fusion | flops 104841216 | bytes 229376 | tf_op jit(solution)/shard_map/while
  361.1 26.5 %multiply_reduce_fusion.6 = f32[128,128]{1,0:T(8,128)S(1)} fusion(f32[128,128]{1,0:T(8,128)S(1)} %copy.91, f32[128]{0:T(128)S(1)} %get-tuple-element.701, f32[128]{0:T(128)S(1)} %get-tuple-element.702, f32[128]{0:T(128)S(1)} %get-tuple-element.703, f32[128]{0:T(128)S(1)} %get-tuple-element.704, f32[128]{0:T(128)S(1)} %get-tuple-element.705, ...), kind=kLoop, calls=%fused_computation.5.clone.1 | loop fusion | flops 104841216 | bytes 229376 | tf_op jit(solution)/shard_map/while
  390.3 26.5 %multiply_reduce_fusion.6 = f32[128,128]{1,0:T(8,128)S(1)} fusion(f32[128,128]{1,0:T(8,128)S(1)} %copy.91, f32[128]{0:T(128)S(1)} %get-tuple-element.701, f32[128]{0:T(128)S(1)} %get-tuple-element.702, f32[128]{0:T(128)S(1)} %get-tuple-element.703, f32[128]{0:T(128)S(1)} %get-tuple-element.704, f32[128]{0:T(128)S(1)} %get-tuple-element.705, ...), kind=kLoop, calls=%fused_computation.5.clone.1 | loop fusion | flops 104841216 | bytes 229376 | tf_op jit(solution)/shard_map/while
  419.5 26.5 %multiply_reduce_fusion.6 = f32[128,128]{1,0:T(8,128)S(1)} fusion(f32[128,128]{1,0:T(8,128)S(1)} %copy.91, f32[128]{0:T(128)S(1)} %get-tuple-element.701, f32[128]{0:T(128)S(1)} %get-tuple-element.702, f32[128]{0:T(128)S(1)} %get-tuple-element.703, f32[128]{0:T(128)S(1)} %get-tuple-element.704, f32[128]{0:T(128)S(1)} %get-tuple-element.705, ...), kind=kLoop, calls=%fused_computation.5.clone.1 | loop fusion | flops 104841216 | bytes 229376 | tf_op jit(solution)/shard_map/while
  448.7 26.5 %multiply_reduce_fusion.6 = f32[128,128]{1,0:T(8,128)S(1)} fusion(f32[128,128]{1,0:T(8,128)S(1)} %copy.91, f32[128]{0:T(128)S(1)} %get-tuple-element.701, f32[128]{0:T(128)S(1)} %get-tuple-element.702, f32[128]{0:T(128)S(1)} %get-tuple-element.703, f32[128]{0:T(128)S(1)} %get-tuple-element.704, f32[128]{0:T(128)S(1)} %get-tuple-element.705, ...), kind=kLoop, calls=%fused_computation.5.clone.1 | loop fusion | flops 104841216 | bytes 229376 | tf_op jit(solution)/shard_map/while
  477.9 26.5 %multiply_reduce_fusion.6 = f32[128,128]{1,0:T(8,128)S(1)} fusion(f32[128,128]{1,0:T(8,128)S(1)} %copy.91, f32[128]{0:T(128)S(1)} %get-tuple-element.701, f32[128]{0:T(128)S(1)} %get-tuple-element.702, f32[128]{0:T(128)S(1)} %get-tuple-element.703, f32[128]{0:T(128)S(1)} %get-tuple-element.704, f32[128]{0:T(128)S(1)} %get-tuple-element.705, ...), kind=kLoop, calls=%fused_computation.5.clone.1 | loop fusion | flops 104841216 | bytes 229376 | tf_op jit(solution)/shard_map/while
  507.0 26.5 %multiply_reduce_fusion.6 = f32[128,128]{1,0:T(8,128)S(1)} fusion(f32[128,128]{1,0:T(8,128)S(1)} %copy.91, f32[128]{0:T(128)S(1)} %get-tuple-element.701, f32[128]{0:T(128)S(1)} %get-tuple-element.702, f32[128]{0:T(128)S(1)} %get-tuple-element.703, f32[128]{0:T(128)S(1)} %get-tuple-element.704, f32[128]{0:T(128)S(1)} %get-tuple-element.705, ...), kind=kLoop, calls=%fused_computation.5.clone.1 | loop fusion | flops 104841216 | bytes 229376 | tf_op jit(solution)/shard_map/while
  536.2 26.5 %multiply_reduce_fusion.6 = f32[128,128]{1,0:T(8,128)S(1)} fusion(f32[128,128]{1,0:T(8,128)S(1)} %copy.91, f32[128]{0:T(128)S(1)} %get-tuple-element.701, f32[128]{0:T(128)S(1)} %get-tuple-element.702, f32[128]{0:T(128)S(1)} %get-tuple-element.703, f32[128]{0:T(128)S(1)} %get-tuple-element.704, f32[128]{0:T(128)S(1)} %get-tuple-element.705, ...), kind=kLoop, calls=%fused_computation.5.clone.1 | loop fusion | flops 104841216 | bytes 229376 | tf_op jit(solution)/shard_map/while
  565.4 26.5 %multiply_reduce_fusion.6 = f32[128,128]{1,0:T(8,128)S(1)} fusion(f32[128,128]{1,0:T(8,128)S(1)} %copy.91, f32[128]{0:T(128)S(1)} %get-tuple-element.701, f32[128]{0:T(128)S(1)} %get-tuple-element.702, f32[128]{0:T(128)S(1)} %get-tuple-element.703, f32[128]{0:T(128)S(1)} %get-tuple-element.704, f32[128]{0:T(128)S(1)} %get-tuple-element.705, ...), kind=kLoop, calls=%fused_computation.5.clone.1 | loop fusion | flops 104841216 | bytes 229376 | tf_op jit(solution)/shard_map/while
  594.6 26.5 %multiply_reduce_fusion.6 = f32[128,128]{1,0:T(8,128)S(1)} fusion(f32[128,128]{1,0:T(8,128)S(1)} %copy.91, f32[128]{0:T(128)S(1)} %get-tuple-element.701, f32[128]{0:T(128)S(1)} %get-tuple-element.702, f32[128]{0:T(128)S(1)} %get-tuple-element.703, f32[128]{0:T(128)S(1)} %get-tuple-element.704, f32[128]{0:T(128)S(1)} %get-tuple-element.705, ...), kind=kLoop, calls=%fused_computation.5.clone.1 | loop fusion | flops 104841216 | bytes 229376 | tf_op jit(solution)/shard_map/while
  623.8 26.5 %multiply_reduce_fusion.6 = f32[128,128]{1,0:T(8,128)S(1)} fusion(f32[128,128]{1,0:T(8,128)S(1)} %copy.91, f32[128]{0:T(128)S(1)} %get-tuple-element.701, f32[128]{0:T(128)S(1)} %get-tuple-element.702, f32[128]{0:T(128)S(1)} %get-tuple-element.703, f32[128]{0:T(128)S(1)} %get-tuple-element.704, f32[128]{0:T(128)S(1)} %get-tuple-element.705, ...), kind=kLoop, calls=%fused_computation.5.clone.1 | loop fusion | flops 104841216 | bytes 229376 | tf_op jit(solution)/shard_map/while
  654.1 1.8 copy.67
  655.9 19.8 %all-gather.4.cloned.1.call-done = f32[8,2048,16]{1,2,0:T(8,128)} async-done(((f32[1,2048,16]{1,2,0:T(8,128)}), f32[8,2048,16]{1,2,0:T(8,128)}) %all-gather.4.cloned.1.call-update) | async-done | bytes 1048592 | tf_op jit(solution)/shard_map/all_gather | solution.py:20
  675.7 9.1 %while.38 = (s32[]{:T(128)}, f32[2048,16]{0,1:T(8,128)S(1)}, s32[]{:T(128)}, f32[8,2048,16]{1,0,2:T(8,128)S(1)}, f32[8,2048,16]{1,2,0:T(8,128)}, /*index=5*/s32[]{:T(128)}, s32[]{:T(128)}) while((s32[]{:T(128)}, f32[2048,16]{0,1:T(8,128)S(1)}, s32[]{:T(128)}, f32[8,2048,16]{1,0,2:T(8,128)S(1)}, f32[8,2048,16]{1,2,0:T(8,128)}, ...), condition=%wide.region_7.8_spmd.clone, body=%wide.region_6.7_spmd.clone.sunk | while | flops 131076 | bytes 786545 | solution.py:32
  675.8 1.0 fusion.194
  676.9 1.0 fusion.194
  678.0 1.0 fusion.194
  679.2 1.0 fusion.194
  680.3 1.0 fusion.194
  681.4 1.0 fusion.194
  682.6 1.0 fusion.194
  683.7 1.0 fusion.194
  684.9 24.7 %while.37 = (s32[]{:T(128)}, f32[16,128,128]{2,1,0:T(8,128)S(1)}, pred[128]{0:T(512)(128)(4,1)S(1)}, f32[16,128,16]{1,0,2:T(8,128)S(1)}, f32[16,128,16]{1,2,0:T(...) while((s32[]{:T(128)}, f32[16,128,128]{2,1,0:T(8,128)S(1)}, pred[128]{0:T(512)(128)(4,1)S(1)}, ...), condition=%wide.region_9.10_spmd, body=%wide.region_8.9_spmd.sunk | while | flops 1050882 | bytes 452193 | solution.py:123
  685.2 1.0 multiply_reduce_fusion.8
  686.8 1.0 multiply_reduce_fusion.8
  688.3 1.0 multiply_reduce_fusion.8
  689.8 1.0 multiply_reduce_fusion.8
  691.4 1.0 multiply_reduce_fusion.8
  692.9 1.0 multiply_reduce_fusion.8
  709.6 1.1 fusion.54
  (518 shorter events, 64.5 us)
Async XLA Ops:
  6.5 647.5 %all-gather.6.cloned.1.call-start = ((), (), s32[]{:S(2)}) async-start(), calls=%async_computation.1 | async-start | bytes 1179648 | tf_op jit(solution)/shard_map/all_gather | solution.py:20
  19.8 3.4 copy-start.4
  19.8 7.5 %copy-start.1 = (bf16[2048,128]{1,0:T(8,128)(2,1)S(1)}, bf16[2048,128]{1,0:T(8,128)(2,1)}, u32[]{:S(2)}) copy-start(bf16[2048,128]{1,0:T(8,128)(2,1)} %param.16) | copy-start | bytes 1572868
  21.2 84.0 %collective-permute-start = (bf16[127,2048]{1,0:T(8,128)(2,1)S(1)}, bf16[127,2048]{1,0:T(8,128)(2,1)S(1)}, u32[]{:S(2)}, u32[]{:S(2)}) collective-permute-start(bf16[127,2048]{1,0:T(8,128)(2,1)S(1)} %slice.1161), channel_id=1, source_target_pairs={{0,4},{4,8},{8,12},{12,16},{16,20},{20,24},{24,28},{1,5},{5,9},{9,... | collective-permute-start | bytes 1560584 | tf_op jit(solution)/shard_map/ppermute | solution.py:15
  23.7 79.3 %collective-permute-start.1 = (s32[1]{0:T(128)}, s32[1]{0:T(128)}, u32[]{:S(2)}, u32[]{:S(2)}) collective-permute-start(s32[1]{0:T(128)} %slice.1127), channel_id=1, source_target_pairs={{0,4},{4,8},{8,12},{12,16},{16,20},{20,24},{24,28},{1,5},{5,9},{9,... | collective-permute-start | bytes 20 | tf_op jit(solution)/shard_map/ppermute | solution.py:15
  94.8 8.2 %copy-start.2 = (f32[2048,16]{0,1:T(8,128)S(1)}, f32[2048,16]{0,1:T(8,128)}, u32[]{:S(2)}) copy-start(f32[2048,16]{0,1:T(8,128)} %param.18) | copy-start | bytes 393220
  94.8 9.6 %copy-start.3 = (f32[2048,16]{0,1:T(8,128)S(1)}, f32[2048,16]{0,1:T(8,128)}, u32[]{:S(2)}) copy-start(f32[2048,16]{0,1:T(8,128)} %param.19) | copy-start | bytes 393220
  105.1 570.5 %all-gather.4.cloned.1.call-start = ((), (), s32[]{:S(2)}) async-start(), calls=%async_computation | async-start | bytes 1179648 | tf_op jit(solution)/shard_map/all_gather | solution.py:20
  134.0 2.4 copy-start.21
  136.4 1.0 copy-start
  136.4 1.0 copy-start.6
  136.4 1.0 copy-start.7
  136.4 1.0 copy-start.8
  136.4 1.0 copy-start.9
  136.4 1.0 copy-start.10
  136.5 1.0 copy-start.11
  136.5 1.0 copy-start.12
  136.5 1.0 copy-start.13
  136.5 1.0 copy-start.14
  136.5 1.0 copy-start.15
  136.5 1.0 copy-start.16
  136.5 1.0 copy-start.17
  136.5 1.0 copy-start.18
  136.5 1.0 copy-start.19
  136.5 1.0 copy-start.20
  137.6 47.8 %copy-start.5 = (f32[2048]{0:T(1024)S(1)}, f32[2048]{0:T(1024)}, u32[]{:S(2)}) copy-start(f32[2048]{0:T(1024)} %param.17) | copy-start | bytes 24580
Sparse Core Ops, SparseCore 0:
  105.3 20.6 all-gather.5
  653.5 22.1 all-gather.3
where the time goes:
time: 727 us; the launch traced here: 718 us
  other arithmetic  549 us (76%)
  local copies, waits for them, and re-layouts  105 us (14%)
  blocking collectives  20.5 us (3%)
  waiting for transfers between devices  19.8 us (3%)
  between operations  15.3 us (2%)
    while x64, other arithmetic  450 us
    slice x7, local copies, waits for them, and re-layouts, depthwise(): total = total + rows * taps_float[:, lag]  75.7 us
    reduce_sum x1, other arithmetic, per_device(): second_total = lax.psum(jnp.sum(first_float * first_float, axis=1), 'chan')  39.2 us
    concatenate x14, other arithmetic, per_device(): widened = jnp.concatenate([earlier_rows, normed])  31.2 us
    all_gather x2, waiting for transfers between devices, entering(): everything = jax.tree.map(lambda part: lax.all_gather(part, axis), array)  19.8 us
  transfers between devices with their start and end apart: 4, of which 1 were waited for; matrix products, arithmetic and copies ran while one was open for 86% of the time, Pallas kernels for 0%

commit v1 on v0

v1 whole, which is shorter than its diff:
```python
from functools import partial

import jax
import jax.numpy as jnp
import numpy as np
from jax import lax
from jax.experimental import pallas as pl
from jax.experimental.pallas import tpu as pltpu
from jax.sharding import PartitionSpec as P

EPSILON = 1e-06
MESH = pl.DeviceIdType.MESH
F32 = jnp.float32
BF16 = jnp.bfloat16
UNROLL = 4


def split_table(table):
    high = table.astype(BF16)
    low = (table - high.astype(np.float64)).astype(BF16)
    return high, low


def dft_tables(rows):
    size = 2 * rows
    k = np.arange(rows)[:, None] + 0.5
    n = np.arange(size)[None, :]
    angle = 2.0 * np.pi * k * n / size
    forward = np.concatenate([np.cos(angle), -np.sin(angle)])
    inverse = (2.0 / size) * forward[:, rows:].T
    return split_table(forward) + split_table(inverse)


def split(x):
    high = x.astype(BF16)
    return high, (x - high.astype(F32)).astype(BF16)


def mm(a, b):
    return jnp.dot(a, b, preferred_element_type=F32)


def mm_nt(a, b):
    return lax.dot_general(a, b, (((1,), (1,)), ((), ())), preferred_element_type=F32)


def kernel(
    n_ctx, n_chan, look, width,
    stream, seg, gain1, taps, gain2, rates, residues, fh, fl, gh, gl,
    out,
    halo, ext, spec, first, xs, ys, dsl, csl, keepb, aliveb,
    part1, part2, sums1, sums2, invs, invr, idb, idr, ends, endr,
    halo_s, halo_r, p1_s, p1_r, p2_s, p2_r, inv_s, inv_r, id_s, id_r, end_s, end_r,
):
    rows, channels = stream.shape
    modes = rates.shape[0]
    chunk = min(256, channels)
    chunks = channels // chunk
    tiles = channels // 128
    group = min(8, tiles)
    halves = tiles // group
    k = lax.axis_index("ctx")
    z = lax.axis_index("chan")

    barrier = pltpu.get_barrier_semaphore()

    def peer(r):
        return {"chan": lax.rem(z + r, n_chan)}

    for r in range(1, n_chan):
        pl.semaphore_signal(barrier, inc=1, device_id=peer(r), device_id_type=MESH)
    for i in range(1, look + 1):
        @pl.when(k + i < n_ctx)
        def _():
            pl.semaphore_signal(barrier, inc=1, device_id={"ctx": k + i}, device_id_type=MESH)

        @pl.when(k >= i)
        def _():
            pl.semaphore_signal(barrier, inc=1, device_id={"ctx": k - i}, device_id_type=MESH)

    eye = lax.broadcasted_iota(jnp.int32, (rows, rows), 0) == lax.broadcasted_iota(
        jnp.int32, (rows, rows), 1
    )

    def to_col(row):
        return jnp.sum(jnp.where(eye, row, 0.0), axis=1, keepdims=True)

    def to_row(col):
        return jnp.sum(jnp.where(eye, col, 0.0), axis=0, keepdims=True)

    def square_step(j, acc):
        x = stream[:, pl.ds(pl.multiple_of(j * 128, 128), 128)].astype(F32)
        return acc + x * x

    acc = lax.fori_loop(0, tiles, square_step, jnp.zeros((rows, 128), F32), unroll=True)
    row = to_row(jnp.sum(acc, axis=1, keepdims=True))
    part1[...] = jnp.broadcast_to(row, part1.shape)
    segf = seg[...].astype(F32)
    lanes = lax.broadcasted_iota(jnp.int32, (1, rows), 1)
    last = jnp.sum(jnp.where(lanes == rows - 1, segf, 0.0), axis=1, keepdims=True)
    idb[...] = jnp.broadcast_to(last, idb.shape)

    peers = n_chan - 1 + jnp.minimum(k, look) + jnp.minimum(n_ctx - 1 - k, look)
    pl.semaphore_wait(barrier, peers)

    def copy(src, dst, s, r, where):
        return pltpu.make_async_remote_copy(
            src_ref=src, dst_ref=dst, send_sem=s, recv_sem=r, device_id=where, device_id_type=MESH
        )

    def sum_copy(part, sums, s, r, i):
        return copy(part, sums.at[i - 1], s.at[i - 1], r.at[i - 1], peer(i))

    def halo_copy(q):
        cols = pl.ds(pl.multiple_of(q * chunk, chunk), chunk)
        return copy(
            stream.at[:, cols], halo.at[:, cols], halo_s.at[q], halo_r.at[q], {"ctx": k + 1}
        )

    def id_copy(i):
        return copy(idb, idr.at[i - 1], id_s.at[i - 1], id_r.at[i - 1], {"ctx": k + i})

    def end_copy(i, h):
        e = (i - 1) * halves + h
        return copy(ends.at[h], endr.at[e], end_s.at[e], end_r.at[e], {"ctx": k + i})

    inv_copy = copy(invs, invr, inv_s, inv_r, {"ctx": k + 1})

    for i in range(1, n_chan):
        sum_copy(part1, sums1, p1_s, p1_r, i).start()

    @pl.when(k + 1 < n_ctx)
    def _():
        for q in range(chunks):
            halo_copy(q).start()

    for i in range(1, look + 1):
        @pl.when(k + i < n_ctx)
        def _():
            id_copy(i).start()

    def spectrum_step(q, c):
        at = pl.ds(pl.multiple_of(q * chunk, chunk), chunk)
        h = taps[at, :]
        spec[:, at] = mm_nt(fh[:, :rows], h) + mm_nt(fl[:, :rows], h)
        return c

    lax.fori_loop(0, chunks, spectrum_step, 0)

    for j in range(tiles):
        at = slice(j * 128, (j + 1) * 128)
        rate = rates[:, at]
        dsl[j * modes : (j + 1) * modes, :] = jnp.exp(-rate)
        doubled = 2.0 * rate
        small = doubled * (1.0 - doubled * (0.5 - doubled * (1.0 / 6.0 - doubled * (1.0 / 24.0 - doubled * (1.0 / 120.0)))))
        gap = jnp.where(doubled < 0.05, small, 1.0 - jnp.exp(-doubled))
        csl[j * modes : (j + 1) * modes, :] = residues[:, at] * jnp.sqrt(gap)
    seg_col = to_col(segf)
    before = lax.broadcasted_iota(jnp.int32, (rows, rows), 0) - 1 == lax.broadcasted_iota(
        jnp.int32, (rows, rows), 1
    )
    prev_col = jnp.sum(jnp.where(before, segf, 0.0), axis=1, keepdims=True)
    keepb[...] = jnp.broadcast_to(jnp.where(seg_col == prev_col, 1.0, 0.0), keepb.shape)

    for i in range(1, n_chan):
        sum_copy(part1, sums1, p1_s, p1_r, i).wait_recv()
    total = part1[...]
    for i in range(1, n_chan):
        total = total + sums1[i - 1]
    full = channels * n_chan
    inverse = lax.rsqrt(total / full + EPSILON)
    invs[...] = inverse

    @pl.when(k + 1 < n_ctx)
    def _():
        inv_copy.start()

    inv_col = to_col(inverse[0:1, :])

    def norm_step(q, c):
        at = pl.ds(pl.multiple_of(q * chunk, chunk), chunk)
        ext[rows:, at] = (stream[:, at].astype(F32) * inv_col * gain1[:, at]).astype(BF16)
        return c

    lax.fori_loop(0, chunks, norm_step, 0)

    @pl.when(k > 0)
    def _():
        inv_copy.wait_recv()

    @pl.when(k == 0)
    def _():
        halo[...] = jnp.zeros_like(halo)
        invr[...] = jnp.zeros_like(invr)

    halo_col = to_col(invr[0:1, :])

    def conv_step(q, acc):
        @pl.when(k > 0)
        def _():
            halo_copy(q).wait_recv()

        at = pl.ds(pl.multiple_of(q * chunk, chunk), chunk)
        ext[:rows, at] = (halo[:, at].astype(F32) * halo_col * gain1[:, at]).astype(BF16)
        x = ext[:, at]
        freq = mm(fh[...], x) + mm(fl[...], x)
        h = spec[:, at]
        xr, xi, hr, hi = freq[:rows], freq[rows:], h[:rows], h[rows:]
        prod = jnp.concatenate([xr * hr - xi * hi, xr * hi + xi * hr], axis=0)
        ph, plow = split(prod)
        mixed = mm(gh[...], ph) + mm(gh[...], plow) + mm(gl[...], ph)
        one = stream[:, at].astype(F32) + x[rows:].astype(F32) * mixed
        one = one.astype(BF16)
        first[:, at] = one
        one = one.astype(F32)
        sq = one * one
        for s in range(chunk // 128):
            acc = acc + sq[:, s * 128 : (s + 1) * 128]
        return acc

    acc = lax.fori_loop(0, chunks, conv_step, jnp.zeros((rows, 128), F32))
    row = to_row(jnp.sum(acc, axis=1, keepdims=True))
    part2[...] = jnp.broadcast_to(row, part2.shape)
    for i in range(1, n_chan):
        sum_copy(part2, sums2, p2_s, p2_r, i).start()
    for i in range(1, look + 1):
        @pl.when(k >= i)
        def _():
            id_copy(i).wait_recv()

    @pl.when(k > 0)
    def _():
        q = idr[0]
        aliveb[...] = jnp.where(seg_col == q[0:1, :], 1.0, 0.0)

    for i in range(1, n_chan):
        sum_copy(part2, sums2, p2_s, p2_r, i).wait_recv()
    total = part2[...]
    for i in range(1, n_chan):
        total = total + sums2[i - 1]
    inv2_col = to_col(lax.rsqrt(total / full + EPSILON)[0:1, :])

    for j in range(tiles):
        at = slice(j * 128, (j + 1) * 128)
        xs[j * rows : (j + 1) * rows, :] = first[:, at].astype(F32) * inv2_col * gain2[:, at]

    def coef_rows(ref, h, m):
        return ref[pl.ds(h * group * modes + m, group, stride=modes), :]

    def time_rows(h, t):
        return pl.ds(h * group * rows + t, group, stride=rows)

    def tree(terms):
        while len(terms) > 1:
            terms = [a + b for a, b in zip(terms[::2], terms[1::2])] + (
                [terms[-1]] if len(terms) % 2 else []
            )
        return terms[0]

    for h in range(halves):
        d = [coef_rows(dsl, h, m) for m in range(modes)]
        c = [coef_rows(csl, h, m) for m in range(modes)]

        def step(b, state):
            for u in range(UNROLL):
                t = b * UNROLL + u
                x = xs[time_rows(h, t), :]
                keep = jnp.broadcast_to(keepb[pl.ds(t, 1), :], x.shape)
                state = [(keep * s) * dm + x for s, dm in zip(state, d)]
                ys[time_rows(h, t), :] = tree([cm * s for cm, s in zip(c, state)])
            return state

        state = lax.fori_loop(0, rows // UNROLL, step, [jnp.zeros((group, 128), F32)] * modes)
        ends[h] = jnp.concatenate(state, axis=0).astype(BF16)
        for i in range(1, look + 1):
            @pl.when(k + i < n_ctx)
            def _():
                end_copy(i, h).start()

    for h in range(halves):
        for i in range(1, look + 1):
            @pl.when(k >= i)
            def _():
                end_copy(i, h).wait_recv()

        @pl.when(k > 0)
        def _():
            d = [coef_rows(dsl, h, m) for m in range(modes)]
            c = [coef_rows(csl, h, m) for m in range(modes)]
            entering = endr[h].astype(F32)
            carried = [entering[m * group : (m + 1) * group] for m in range(modes)]
            powers = list(d)
            hops = 1
            while hops < rows:
                powers = [p * p for p in powers]
                hops *= 2
            decay = powers
            for i in range(2, look + 1):
                same = jnp.where(idr[i - 1] == idr[0], 1.0, 0.0)[:group]
                same = jnp.where(k >= i, same, 0.0)
                old = endr[(i - 1) * halves + h].astype(F32)
                carried = [
                    a + jnp.where(same > 0.0, p * old[m * group : (m + 1) * group], 0.0)
                    for m, (a, p) in enumerate(zip(carried, decay))
                ]
                decay = [p * q for p, q in zip(decay, powers)]
            lead = [cm * dm * s for cm, dm, s in zip(c, d, carried)]

            def step(b, lead):
                for u in range(UNROLL):
                    t = b * UNROLL + u
                    at = time_rows(h, t)
                    alive = jnp.broadcast_to(aliveb[pl.ds(t, 1), :], (group, 128))
                    ys[at, :] = ys[at, :] + alive * tree(lead)
                    lead = [p * dm for p, dm in zip(lead, d)]
                return lead

            lax.fori_loop(0, rows // UNROLL, step, lead)

        for j in range(h * group, (h + 1) * group):
            at = slice(j * 128, (j + 1) * 128)
            slab = slice(j * rows, (j + 1) * rows)
            out[:, at] = (first[:, at].astype(F32) + xs[slab, :] * ys[slab, :]).astype(BF16)

    for i in range(1, n_chan):
        sum_copy(part1, sums1, p1_s, p1_r, i).wait_send()
        sum_copy(part2, sums2, p2_s, p2_r, i).wait_send()

    @pl.when(k + 1 < n_ctx)
    def _():
        inv_copy.wait_send()
        for q in range(chunks):
            halo_copy(q).wait_send()

    for i in range(1, look + 1):
        @pl.when(k + i < n_ctx)
        def _():
            id_copy(i).wait_send()
            for h in range(halves):
                end_copy(i, h).wait_send()


def per_device(stream, seg_ids, mr_gain, mr_filter, li_gain, decay_rates, residues):
    rows, channels = stream.shape
    modes = decay_rates.shape[1]
    n_ctx, n_chan = lax.axis_size("ctx"), lax.axis_size("chan")
    assert rows == mr_filter.shape[1]
    longest = rows * n_ctx // 4
    look = max(1, min(n_ctx - 1, -(-(longest - 1) // rows)))
    tiles = channels // 128
    group = min(8, tiles)
    halves = tiles // group
    chunks = channels // min(256, channels)
    vmem = pl.BlockSpec(memory_space=pltpu.VMEM)
    dma = pltpu.SemaphoreType.DMA
    others = max(1, n_chan - 1)
    small = (8, 128)
    tables = [jnp.asarray(t) for t in dft_tables(rows)]
    return pl.pallas_call(
        partial(kernel, n_ctx, n_chan, look, channels),
        out_shape=jax.ShapeDtypeStruct((rows, channels), BF16),
        in_specs=[vmem] * 11,
        out_specs=vmem,
        scratch_shapes=[
            pltpu.VMEM((rows, channels), BF16),
            pltpu.VMEM((2 * rows, channels), BF16),
            pltpu.VMEM((2 * rows, channels), F32),
            pltpu.VMEM((rows, channels), BF16),
            pltpu.VMEM((tiles * rows, 128), F32),
            pltpu.VMEM((tiles * rows, 128), F32),
            pltpu.VMEM((tiles * modes, 128), F32),
            pltpu.VMEM((tiles * modes, 128), F32),
            pltpu.VMEM((rows, 128), F32),
            pltpu.VMEM((rows, 128), F32),
            pltpu.VMEM(small, F32),
            pltpu.VMEM(small, F32),
            pltpu.VMEM((others,) + small, F32),
            pltpu.VMEM((others,) + small, F32),
            pltpu.VMEM(small, F32),
            pltpu.VMEM(small, F32),
            pltpu.VMEM(small, F32),
            pltpu.VMEM((look,) + small, F32),
            pltpu.VMEM((halves, modes * group, 128), BF16),
            pltpu.VMEM((look * halves, modes * group, 128), BF16),
            dma((chunks,)), dma((chunks,)),
            dma((others,)), dma((others,)),
            dma((others,)), dma((others,)),
            dma, dma,
            dma((look,)), dma((look,)),
            dma((look * halves,)), dma((look * halves,)),
        ],
        compiler_params=pltpu.CompilerParams(
            collective_id=0, has_side_effects=True, vmem_limit_bytes=40 * 2**20
        ),
    )(
        stream, seg_ids.reshape(1, rows), mr_gain.reshape(1, channels), mr_filter,
        li_gain.reshape(1, channels), decay_rates.T, residues.T, *tables,
    )


def solution(mesh):
    placed = (
        P("ctx", "chan"),
        P("ctx"),
        P("chan"),
        P("chan", None),
        P("chan"),
        P("chan", None),
        P("chan", None),
    )
    return jax.shard_map(
        per_device, mesh=mesh, in_specs=placed, out_specs=P("ctx", "chan"), check_vma=False
    )
```

time: 727 us -> 37.5 us (0.05); the launches traced: 718 us -> 37.1 us
  other arithmetic: 549 us -> 0 us
  local copies, waits for them, and re-layouts: 105 us -> 9.57 us
  Pallas kernels: 0 us -> 27.5 us
  blocking collectives: 20.5 us -> 0 us
  waiting for transfers between devices: 19.8 us -> 0 us
  between operations: 15.3 us -> 0.02 us
    while x64 -> x0, other arithmetic: 450 us -> none
    slice x25 -> x0, local copies, waits for them, and re-layouts: 85.7 us -> none  [the longest x7 75.7 us: depthwise(): total = total + rows * taps_float[:, lag]]
    reduce_sum x2 -> x0, other arithmetic: 40.4 us -> none  [the longest x1 39.2 us: per_device(): second_total = lax.psum(jnp.sum(first_float * first_float, axis=1), 'chan')]
    concatenate x14 -> x0, other arithmetic: 31.2 us -> none  [per_device(): widened = jnp.concatenate([earlier_rows, normed])]
    pallas_call x0 -> x1, Pallas kernels: none -> 27.5 us  [per_device(): pl.pallas_call(partial(kernel, n_ctx, n_chan, look, channels), out_shape=...]
    psum x2 -> x0, blocking collectives: 20.5 us -> none  [the longest x1 12 us: per_device(): sum_total = lax.psum(squares, 'chan')]
    all_gather x2 -> x0, waiting for transfers between devices: 19.8 us -> none  [entering(): everything = jax.tree.map(lambda part: lax.all_gather(part, axis), array)]
    eq x17 -> x0, other arithmetic: 11 us -> none  [the longest x16 10.4 us: local_pass(): ending = seg_ids == seg_ids[block_size - 1]]
  transfers between devices with their start and end apart: 4 -> 0, of which waited for: 1 -> 0; matrix products, arithmetic and copies ran while one was open for 86% -> 0% of each run, Pallas kernels for 0% -> 0%
where the time goes in v1:
time: 37.5 us; the launch traced here: 37.1 us
  Pallas kernels  27.5 us (73%)
  local copies, waits for them, and re-layouts  9.57 us (26%)
    pallas_call x1, Pallas kernels, per_device(): pl.pallas_call(partial(kernel, n_ctx, n_chan, look, channels), out_shape=...  27.5 us
    unnamed x23, local copies, waits for them, and re-layouts  9.57 us

profile of v1, /device:TPU:4, one launch (start us, length us, event | category | flops | bytes accessed | tf_op | source)
XLA Modules:
  0.0 37.1 jit_solution(11597853768812856787)
XLA Ops:
  0.0 0.0 copy-start.8
  0.0 0.0 copy-start.10
  0.0 0.7 %copy-done.8 = f32[2048]{0:T(1024)S(1)} copy-done((f32[2048]{0:T(1024)S(1)}, f32[2048]{0:T(1024)}, u32[]{:S(2)}) %copy-start.8) | copy-done | bytes 8216
  0.7 0.0 copy-done.10
  0.7 0.0 copy-start
  0.7 1.0 %copy-done = bf16[128,2048]{1,0:T(8,128)(2,1)S(1)} copy-done((bf16[128,2048]{1,0:T(8,128)(2,1)S(1)}, bf16[128,2048]{1,0:T(8,128)(2,1)}, u32[]{:S(2)}) %copy-start) | copy-done | bytes 524312
  1.7 0.0 copy-start.1
  1.7 1.0 %copy-done.1 = bf16[2048,128]{1,0:T(8,128)(2,1)S(1)} copy-done((bf16[2048,128]{1,0:T(8,128)(2,1)S(1)}, bf16[2048,128]{1,0:T(8,128)(2,1)}, u32[]{:S(2)}) %copy-start.1) | copy-done | bytes 524312
  2.8 0.0 copy-start.2
  2.8 0.9 %copy-done.2 = f32[2048,16]{0,1:T(8,128)S(1)} copy-done((f32[2048,16]{0,1:T(8,128)S(1)}, f32[2048,16]{0,1:T(8,128)}, u32[]{:S(2)}) %copy-start.2) | copy-done | bytes 131096
  3.7 0.0 copy-start.3
  3.7 0.9 %copy-done.3 = f32[2048,16]{0,1:T(8,128)S(1)} copy-done((f32[2048,16]{0,1:T(8,128)S(1)}, f32[2048,16]{0,1:T(8,128)}, u32[]{:S(2)}) %copy-start.3) | copy-done | bytes 131096
  4.6 0.0 copy-start.4
  4.6 0.9 %copy-done.4 = bf16[256,256]{1,0:T(8,128)(2,1)S(1)} copy-done((bf16[256,256]{1,0:T(8,128)(2,1)S(1)}, bf16[256,256]{1,0:T(8,128)(2,1)}, u32[]{:S(2)}) %copy-start.4) | copy-done | bytes 131096
  5.5 0.0 copy-start.5
  5.5 0.9 %copy-done.5 = bf16[256,256]{1,0:T(8,128)(2,1)S(1)} copy-done((bf16[256,256]{1,0:T(8,128)(2,1)S(1)}, bf16[256,256]{1,0:T(8,128)(2,1)}, u32[]{:S(2)}) %copy-start.5) | copy-done | bytes 131096
  6.4 0.0 copy-start.6
  6.4 0.8 %copy-done.6 = bf16[128,256]{1,0:T(8,128)(2,1)S(1)} copy-done((bf16[128,256]{1,0:T(8,128)(2,1)S(1)}, bf16[128,256]{1,0:T(8,128)(2,1)}, u32[]{:S(2)}) %copy-start.6) | copy-done | bytes 65560
  7.2 0.0 copy-start.7
  7.2 0.8 %copy-done.7 = bf16[128,256]{1,0:T(8,128)(2,1)S(1)} copy-done((bf16[128,256]{1,0:T(8,128)(2,1)S(1)}, bf16[128,256]{1,0:T(8,128)(2,1)}, u32[]{:S(2)}) %copy-start.7) | copy-done | bytes 65560
  8.1 0.0 copy-start.9
  8.1 0.7 %copy-done.9 = f32[2048]{0:T(1024)S(1)} copy-done((f32[2048]{0:T(1024)S(1)}, f32[2048]{0:T(1024)}, u32[]{:S(2)}) %copy-start.9) | copy-done | bytes 8216
  8.8 27.5 %shard_map.109 = bf16[128,2048]{1,0:T(8,128)(2,1)S(1)} custom-call(bf16[128,2048]{1,0:T(8,128)(2,1)S(1)} %copy-done, s32[1,128]{1,0:T(1,128)S(1)} %bitcast.9, f32[1,2048]{1,0:T(1,128)S(1)} %bitcast.7, bf16[2048,128]{1,0:T(8,128)(2,1)S(1)} %copy-done.1, f32[1,2048]{1,0:T(1,128)S(1)} %bitcast.8, f32[16,2048]{1,0:T(8,128)S(1)} %bitcast.5, ...), custom_call_target="tpu_custom_call" | custom-call | tf_op jit(solution)/shard_map/pallas_call | solution.py:359
  36.3 0.8 %copy.13 = bf16[128,2048]{1,0:T(8,128)(2,1)} copy(bf16[128,2048]{1,0:T(8,128)(2,1)S(1)} %shard_map.109) | data formatting | bytes 1048576
Async XLA Ops:
  0.0 0.7 %copy-start.8 = (f32[2048]{0:T(1024)S(1)}, f32[2048]{0:T(1024)}, u32[]{:S(2)}) copy-start(f32[2048]{0:T(1024)} %param.13) | copy-start | bytes 24580
  0.0 0.7 %copy-start.10 = (s32[128]{0:T(128)S(1)}, s32[128]{0:T(128)}, u32[]{:S(2)}) copy-start(s32[128]{0:T(128)} %param.12) | copy-start | bytes 1540
  0.7 1.0 %copy-start = (bf16[128,2048]{1,0:T(8,128)(2,1)S(1)}, bf16[128,2048]{1,0:T(8,128)(2,1)}, u32[]{:S(2)}) copy-start(bf16[128,2048]{1,0:T(8,128)(2,1)} %stream.1) | copy-start | bytes 1572868
  1.7 1.0 %copy-start.1 = (bf16[2048,128]{1,0:T(8,128)(2,1)S(1)}, bf16[2048,128]{1,0:T(8,128)(2,1)}, u32[]{:S(2)}) copy-start(bf16[2048,128]{1,0:T(8,128)(2,1)} %taps.1) | copy-start | bytes 1572868
  2.8 0.9 %copy-start.2 = (f32[2048,16]{0,1:T(8,128)S(1)}, f32[2048,16]{0,1:T(8,128)}, u32[]{:S(2)}) copy-start(f32[2048,16]{0,1:T(8,128)} %param.16) | copy-start | bytes 393220
  3.7 0.9 %copy-start.3 = (f32[2048,16]{0,1:T(8,128)S(1)}, f32[2048,16]{0,1:T(8,128)}, u32[]{:S(2)}) copy-start(f32[2048,16]{0,1:T(8,128)} %param.17) | copy-start | bytes 393220
  4.6 0.9 %copy-start.4 = (bf16[256,256]{1,0:T(8,128)(2,1)S(1)}, bf16[256,256]{1,0:T(8,128)(2,1)}, u32[]{:S(2)}) copy-start(bf16[256,256]{1,0:T(8,128)(2,1)} %constant.9.clone.fl) | copy-start | bytes 393220
  5.5 0.9 %copy-start.5 = (bf16[256,256]{1,0:T(8,128)(2,1)S(1)}, bf16[256,256]{1,0:T(8,128)(2,1)}, u32[]{:S(2)}) copy-start(bf16[256,256]{1,0:T(8,128)(2,1)} %constant.8.clone.fh) | copy-start | bytes 393220
  6.4 0.8 %copy-start.6 = (bf16[128,256]{1,0:T(8,128)(2,1)S(1)}, bf16[128,256]{1,0:T(8,128)(2,1)}, u32[]{:S(2)}) copy-start(bf16[128,256]{1,0:T(8,128)(2,1)} %constant.11.clone.gl) | copy-start | bytes 196612
  7.2 0.8 %copy-start.7 = (bf16[128,256]{1,0:T(8,128)(2,1)S(1)}, bf16[128,256]{1,0:T(8,128)(2,1)}, u32[]{:S(2)}) copy-start(bf16[128,256]{1,0:T(8,128)(2,1)} %constant.10.clone.gh) | copy-start | bytes 196612
  8.1 0.7 %copy-start.9 = (f32[2048]{0:T(1024)S(1)}, f32[2048]{0:T(1024)}, u32[]{:S(2)}) copy-start(f32[2048]{0:T(1024)} %param.15) | copy-start | bytes 24580

commit v2 on v1

--- a/solution.py
+++ b/solution.py
@@ -46,12 +46,21 @@
 
 def kernel(
     n_ctx, n_chan, look, width,
-    stream, seg, gain1, taps, gain2, rates, residues, fh, fl, gh, gl,
-    out,
-    halo, ext, spec, first, xs, ys, dsl, csl, keepb, aliveb,
-    part1, part2, sums1, sums2, invs, invr, idb, idr, ends, endr,
-    halo_s, halo_r, p1_s, p1_r, p2_s, p2_r, inv_s, inv_r, id_s, id_r, end_s, end_r,
+    *refs,
 ):
+    sources, out, held, load_sem = refs[:11], refs[11], refs[12:23], refs[23]
+    (
+        halo, ext, spec, first, xs, ys, dsl, csl, keepb, aliveb,
+        part1, part2, sums1, sums2, invs, invr, idb, idr, ends, endr,
+        halo_s, halo_r, p1_s, p1_r, p2_s, p2_r, inv_s, inv_r, id_s, id_r, end_s, end_r,
+    ) = refs[24:]
+    stream, seg, gain1, taps, gain2, rates, residues, fh, fl, gh, gl = held
+    loads = [
+        pltpu.make_async_copy(source, target, load_sem.at[i])
+        for i, (source, target) in enumerate(zip(sources, held))
+    ]
+    for i in (0, 1, 7, 8, 3, 5, 6, 2, 9, 10, 4):
+        loads[i].start()
     rows, channels = stream.shape
     modes = rates.shape[0]
     chunk = min(256, channels)
@@ -88,6 +97,9 @@
     def to_row(col):
         return jnp.sum(jnp.where(eye, col, 0.0), axis=0, keepdims=True)
 
+    loads[0].wait()
+    loads[1].wait()
+
     def square_step(j, acc):
         x = stream[:, pl.ds(pl.multiple_of(j * 128, 128), 128)].astype(F32)
         return acc + x * x
@@ -114,7 +126,7 @@
     def halo_copy(q):
         cols = pl.ds(pl.multiple_of(q * chunk, chunk), chunk)
         return copy(
-            stream.at[:, cols], halo.at[:, cols], halo_s.at[q], halo_r.at[q], {"ctx": k + 1}
+            sources[0].at[:, cols], halo.at[:, cols], halo_s.at[q], halo_r.at[q], {"ctx": k + 1}
         )
 
     def id_copy(i):
@@ -138,6 +150,9 @@
         @pl.when(k + i < n_ctx)
         def _():
             id_copy(i).start()
+
+    for i in (7, 8, 3):
+        loads[i].wait()
 
     def spectrum_step(q, c):
         at = pl.ds(pl.multiple_of(q * chunk, chunk), chunk)
@@ -146,6 +161,9 @@
         return c
 
     lax.fori_loop(0, chunks, spectrum_step, 0)
+
+    for i in (5, 6, 2, 9, 10, 4):
+        loads[i].wait()
 
     for j in range(tiles):
         at = slice(j * 128, (j + 1) * 128)
@@ -356,12 +374,18 @@
     others = max(1, n_chan - 1)
     small = (8, 128)
     tables = [jnp.asarray(t) for t in dft_tables(rows)]
+    operands = (
+        stream, seg_ids.reshape(1, rows), mr_gain.reshape(1, channels), mr_filter,
+        li_gain.reshape(1, channels), decay_rates.T, residues.T, *tables,
+    )
     return pl.pallas_call(
         partial(kernel, n_ctx, n_chan, look, channels),
         out_shape=jax.ShapeDtypeStruct((rows, channels), BF16),
-        in_specs=[vmem] * 11,
+        in_specs=[pl.BlockSpec(memory_space=pltpu.HBM)] * len(operands),
         out_specs=vmem,
-        scratch_shapes=[
+        scratch_shapes=[pltpu.VMEM(x.shape, x.dtype) for x in operands]
+        + [
+            dma((len(operands),)),
             pltpu.VMEM((rows, channels), BF16),
             pltpu.VMEM((2 * rows, channels), BF16),
             pltpu.VMEM((2 * rows, channels), F32),
@@ -390,12 +414,9 @@
             dma((look * halves,)), dma((look * halves,)),
         ],
         compiler_params=pltpu.CompilerParams(
-            collective_id=0, has_side_effects=True, vmem_limit_bytes=40 * 2**20
+            collective_id=0, has_side_effects=True, vmem_limit_bytes=62 * 2**20
         ),
-    )(
-        stream, seg_ids.reshape(1, rows), mr_gain.reshape(1, channels), mr_filter,
-        li_gain.reshape(1, channels), decay_rates.T, residues.T, *tables,
-    )
+    )(*operands)
 
 
 def solution(mesh):

time: 37.5 us -> 30.7 us (0.82)
  local copies, waits for them, and re-layouts: 9.57 us -> 1.88 us
  Pallas kernels: 27.5 us -> 28.6 us
    unnamed x23 -> x1, local copies, waits for them, and re-layouts: 9.57 us -> 1.88 us
    pallas_call x1, Pallas kernels: 27.5 us -> 28.6 us  [per_device(): pl.pallas_call(partial(kernel, n_ctx, n_chan, look, channels), out_shape=...]
where the time goes in v2:
time: 30.7 us; the launch traced here: 30.5 us
  Pallas kernels  28.6 us (93%)
  local copies, waits for them, and re-layouts  1.88 us (6%)
    pallas_call x1, Pallas kernels, per_device(): pl.pallas_call(partial(kernel, n_ctx, n_chan, look, channels), out_shape=...  28.6 us
    unnamed x1, local copies, waits for them, and re-layouts  1.88 us

profile of v2, /device:TPU:4, one launch (start us, length us, event | category | flops | bytes accessed | tf_op | source)
XLA Modules:
  0.0 30.5 jit_solution(18430586691664196643)
XLA Ops:
  0.0 28.6 %shard_map.109 = bf16[128,2048]{1,0:T(8,128)(2,1)} custom-call(bf16[128,2048]{1,0:T(8,128)(2,1)} %refs_0_.1, s32[1,128]{1,0:T(1,128)} %bitcast.9, f32[1,2048]{1,0:T(1,128)} %bitcast.7, bf16[2048,128]{1,0:T(8,128)(2,1)} %refs_3_.1, f32[1,2048]{1,0:T(1,128)} %bitcast.8, f32[16,2048]{1,0:T(8,128)} %bitcast.5, f32[16,2048]{1,0:T(8,128)} %bitcast.6, ...), custom_call_target="tpu_custom_call" | custom-call | tf_op jit(solution)/shard_map/pallas_call | solution.py:381
  28.6 1.9 %copy.13 = bf16[128,2048]{1,0:T(8,128)(2,1)} copy(bf16[128,2048]{1,0:T(8,128)(2,1)} %shard_map.109) | data formatting | bytes 1048576

commit v3 on v2

--- a/solution.py
+++ b/solution.py
@@ -13,6 +13,7 @@
 F32 = jnp.float32
 BF16 = jnp.bfloat16
 UNROLL = 4
+PAD = 8
 
 
 def split_table(table):
@@ -68,6 +69,7 @@
     tiles = channels // 128
     group = min(8, tiles)
     halves = tiles // group
+    pitch = rows + PAD
     k = lax.axis_index("ctx")
     z = lax.axis_index("chan")
 
@@ -260,13 +262,13 @@
 
     for j in range(tiles):
         at = slice(j * 128, (j + 1) * 128)
-        xs[j * rows : (j + 1) * rows, :] = first[:, at].astype(F32) * inv2_col * gain2[:, at]
+        xs[j * pitch : j * pitch + rows, :] = first[:, at].astype(F32) * inv2_col * gain2[:, at]
 
     def coef_rows(ref, h, m):
         return ref[pl.ds(h * group * modes + m, group, stride=modes), :]
 
     def time_rows(h, t):
-        return pl.ds(h * group * rows + t, group, stride=rows)
+        return pl.ds(h * group * pitch + t, group, stride=pitch)
 
     def tree(terms):
         while len(terms) > 1:
@@ -337,7 +339,7 @@
 
         for j in range(h * group, (h + 1) * group):
             at = slice(j * 128, (j + 1) * 128)
-            slab = slice(j * rows, (j + 1) * rows)
+            slab = slice(j * pitch, j * pitch + rows)
             out[:, at] = (first[:, at].astype(F32) + xs[slab, :] * ys[slab, :]).astype(BF16)
 
     for i in range(1, n_chan):
@@ -390,8 +392,8 @@
             pltpu.VMEM((2 * rows, channels), BF16),
             pltpu.VMEM((2 * rows, channels), F32),
             pltpu.VMEM((rows, channels), BF16),
-            pltpu.VMEM((tiles * rows, 128), F32),
-            pltpu.VMEM((tiles * rows, 128), F32),
+            pltpu.VMEM((tiles * (rows + PAD), 128), F32),
+            pltpu.VMEM((tiles * (rows + PAD), 128), F32),
             pltpu.VMEM((tiles * modes, 128), F32),
             pltpu.VMEM((tiles * modes, 128), F32),
             pltpu.VMEM((rows, 128), F32),

time: 30.7 us -> 29.8 us (0.971)
  Pallas kernels: 28.6 us -> 27.8 us
    pallas_call x1, Pallas kernels: 28.6 us -> 27.8 us  [per_device(): pl.pallas_call(partial(kernel, n_ctx, n_chan, look, channels), out_shape=...]
where the time goes in v3:
time: 29.8 us; the launch traced here: 29.6 us
  Pallas kernels  27.8 us (93%)
  local copies, waits for them, and re-layouts  1.88 us (6%)
    pallas_call x1, Pallas kernels, per_device(): pl.pallas_call(partial(kernel, n_ctx, n_chan, look, channels), out_shape=...  27.8 us
    unnamed x1, local copies, waits for them, and re-layouts  1.88 us

profile of v3, /device:TPU:4, one launch (start us, length us, event | category | flops | bytes accessed | tf_op | source)
XLA Modules:
  0.0 29.6 jit_solution(6118759981933617845)
XLA Ops:
  0.0 27.8 %shard_map.109 = bf16[128,2048]{1,0:T(8,128)(2,1)} custom-call(bf16[128,2048]{1,0:T(8,128)(2,1)} %refs_0_.1, s32[1,128]{1,0:T(1,128)} %bitcast.9, f32[1,2048]{1,0:T(1,128)} %bitcast.7, bf16[2048,128]{1,0:T(8,128)(2,1)} %refs_3_.1, f32[1,2048]{1,0:T(1,128)} %bitcast.8, f32[16,2048]{1,0:T(8,128)} %bitcast.5, f32[16,2048]{1,0:T(8,128)} %bitcast.6, ...), custom_call_target="tpu_custom_call" | custom-call | tf_op jit(solution)/shard_map/pallas_call | solution.py:383
  27.8 1.9 %copy.13 = bf16[128,2048]{1,0:T(8,128)(2,1)} copy(bf16[128,2048]{1,0:T(8,128)(2,1)} %shard_map.109) | data formatting | bytes 1048576

commit v4 on v3

--- a/solution.py
+++ b/solution.py
@@ -12,7 +12,7 @@
 MESH = pl.DeviceIdType.MESH
 F32 = jnp.float32
 BF16 = jnp.bfloat16
-UNROLL = 4
+UNROLL = 8
 PAD = 8
 
 
@@ -382,7 +382,7 @@
     )
     return pl.pallas_call(
         partial(kernel, n_ctx, n_chan, look, channels),
-        out_shape=jax.ShapeDtypeStruct((rows, channels), BF16),
+        out_shape=pltpu.VMEM((rows, channels), BF16),
         in_specs=[pl.BlockSpec(memory_space=pltpu.HBM)] * len(operands),
         out_specs=vmem,
         scratch_shapes=[pltpu.VMEM(x.shape, x.dtype) for x in operands]
@@ -416,7 +416,7 @@
             dma((look * halves,)), dma((look * halves,)),
         ],
         compiler_params=pltpu.CompilerParams(
-            collective_id=0, has_side_effects=True, vmem_limit_bytes=62 * 2**20
+            collective_id=0, has_side_effects=True, vmem_limit_bytes=56 * 2**20
         ),
     )(*operands)
 

time: 29.8 us -> 27.6 us (0.926)
  Pallas kernels: 27.8 us -> 26.7 us
  local copies, waits for them, and re-layouts: 1.88 us -> 0.8 us
    unnamed x1, local copies, waits for them, and re-layouts: 1.88 us -> 0.8 us
    pallas_call x1, Pallas kernels: 27.8 us -> 26.7 us  [per_device(): pl.pallas_call(partial(kernel, n_ctx, n_chan, look, channels), out_shape=...]
where the time goes in v4:
time: 27.6 us; the launch traced here: 27.5 us
  Pallas kernels  26.7 us (97%)
  local copies, waits for them, and re-layouts  0.8 us (3%)
    pallas_call x1, Pallas kernels, per_device(): pl.pallas_call(partial(kernel, n_ctx, n_chan, look, channels), out_shape=...  26.7 us
    unnamed x1, local copies, waits for them, and re-layouts  0.8 us

profile of v4, /device:TPU:4, one launch (start us, length us, event | category | flops | bytes accessed | tf_op | source)
XLA Modules:
  0.0 27.5 jit_solution(7064685271564904032)
XLA Ops:
  0.0 26.7 %shard_map.109 = bf16[128,2048]{1,0:T(8,128)(2,1)S(1)} custom-call(bf16[128,2048]{1,0:T(8,128)(2,1)} %refs_0_.1, s32[1,128]{1,0:T(1,128)} %bitcast.9, f32[1,2048]{1,0:T(1,128)} %bitcast.7, bf16[2048,128]{1,0:T(8,128)(2,1)} %refs_3_.1, f32[1,2048]{1,0:T(1,128)} %bitcast.8, f32[16,2048]{1,0:T(8,128)} %bitcast.5, f32[16,2048]{1,0:T(8,128)} %bitcast.6, ...), custom_call_target="tpu_custom_call" | custom-call | tf_op jit(solution)/shard_map/pallas_call | solution.py:383
  26.7 0.8 %copy.13 = bf16[128,2048]{1,0:T(8,128)(2,1)} copy(bf16[128,2048]{1,0:T(8,128)(2,1)S(1)} %shard_map.109) | data formatting | bytes 1048576

commit v5 on v4

--- a/solution.py
+++ b/solution.py
@@ -64,7 +64,7 @@
         loads[i].start()
     rows, channels = stream.shape
     modes = rates.shape[0]
-    chunk = min(256, channels)
+    chunk = min(512, channels)
     chunks = channels // chunk
     tiles = channels // 128
     group = min(8, tiles)
@@ -370,7 +370,7 @@
     tiles = channels // 128
     group = min(8, tiles)
     halves = tiles // group
-    chunks = channels // min(256, channels)
+    chunks = channels // min(512, channels)
     vmem = pl.BlockSpec(memory_space=pltpu.VMEM)
     dma = pltpu.SemaphoreType.DMA
     others = max(1, n_chan - 1)

time: 27.6 us -> 25.8 us (0.935)
  Pallas kernels: 26.7 us -> 24.9 us
    pallas_call x1, Pallas kernels: 26.7 us -> 24.9 us  [per_device(): pl.pallas_call(partial(kernel, n_ctx, n_chan, look, channels), out_shape=...]
where the time goes in v5:
time: 25.8 us; the launch traced here: 25.7 us
  Pallas kernels  24.9 us (97%)
  local copies, waits for them, and re-layouts  0.8 us (3%)
    pallas_call x1, Pallas kernels, per_device(): pl.pallas_call(partial(kernel, n_ctx, n_chan, look, channels), out_shape=...  24.9 us
    unnamed x1, local copies, waits for them, and re-layouts  0.8 us

profile of v5, /device:TPU:4, one launch (start us, length us, event | category | flops | bytes accessed | tf_op | source)
XLA Modules:
  0.0 25.7 jit_solution(17312335388915331408)
XLA Ops:
  0.0 24.9 %shard_map.109 = bf16[128,2048]{1,0:T(8,128)(2,1)S(1)} custom-call(bf16[128,2048]{1,0:T(8,128)(2,1)} %refs_0_.1, s32[1,128]{1,0:T(1,128)} %bitcast.9, f32[1,2048]{1,0:T(1,128)} %bitcast.7, bf16[2048,128]{1,0:T(8,128)(2,1)} %refs_3_.1, f32[1,2048]{1,0:T(1,128)} %bitcast.8, f32[16,2048]{1,0:T(8,128)} %bitcast.5, f32[16,2048]{1,0:T(8,128)} %bitcast.6, ...), custom_call_target="tpu_custom_call" | custom-call | tf_op jit(solution)/shard_map/pallas_call | solution.py:383
  24.9 0.8 %copy.13 = bf16[128,2048]{1,0:T(8,128)(2,1)} copy(bf16[128,2048]{1,0:T(8,128)(2,1)S(1)} %shard_map.109) | data formatting | bytes 1048576
